TPU v7x, 32 devices: a whole 2x2x4 slice. The times are simulated.
32 devices in a mesh: group: 4 (over y, x), mp: 8 (over z, core).
Axes of the slice: x: 2, y: 2, z: 4, core: 2. Of those that a mesh axis runs over, the one named last changes fastest.
Arguments:
- inputs: bfloat16 [2, 3072, 8192], P(None, 'group', 'mp'), may hold values from -6 to 6
- targets: bfloat16 [2, 3072, 1024], P(None, ('group', 'mp')), may hold values from -6 to 6
- numerator: bfloat16 [4, 8192, 1024], P('group', 'mp'), may hold values from -6 to 6
- momentum: float32 [4, 8192, 1024], P('group', 'mp'), may hold values from -4 to 4
- received: bfloat16 [4, 8192, 1024], P('group', 'mp'), may hold values from -6 to 6
- push_weight: float32 [4], P('group'), may hold values from 0.5 to 2
- received_weight: float32 [4], P('group'), may hold values from 0.5 to 2
- mix_share: int32 [4, 2], P('group'), may hold values from 1 to 7
Outputs:
- final_numerator: bfloat16 [4, 8192, 1024], P('group', 'mp')
- final_weight: float32 [4], P('group')
- final_received: bfloat16 [4, 8192, 1024], P('group', 'mp')
- final_received_weight: float32 [4], P('group')
- value_rows: bfloat16 [2, 3072, 1024], P(None, ('group', 'mp'))
All inputs are finite; a program needn't handle non-finite values.
Results may differ from a plain program's by a relative error of at most 0.02.
Values may be sent and summed in bfloat16 or wider, within the bound.
A program may use at most 64 MiB of HBM per device.

v0:
```python
import math

import jax
import jax.numpy as jnp
from jax import lax
from jax.sharding import PartitionSpec as P

D = 8192
TOK_GRP = 768


momentum_decay = 0.9
step_size = 0.5


def from_behind(value, axis, steps):
    count = lax.axis_size(axis)
    pairs = [(source, (source + steps) % count) for source in range(count)]
    return lax.ppermute(value, axis, pairs)


def local(inputs, targets, numerator, momentum, received, push_weight, received_weight, mix_share):
    row_scale = 1.0 / math.sqrt(D)
    grad_scale = 1.0 / math.sqrt(TOK_GRP)
    steps_count = inputs.shape[0]
    own_rows = targets.shape[1]
    current = numerator[0]
    velocity = momentum[0]
    arrived = received[0]
    arrived_weight = received_weight
    weight = push_weight
    value_steps = []
    for step_index in range(steps_count):
        tokens = inputs[step_index]
        scaled = (current.astype(jnp.float32) / weight[0]).astype(jnp.bfloat16)

        def row_term(first_row, row_count, tokens=tokens, scaled=scaled):
            product = jnp.dot(tokens, scaled, preferred_element_type=jnp.float32) * row_scale
            return lax.optimization_barrier(product.astype(jnp.bfloat16)).astype(jnp.float32)

        values = lax.psum_scatter(
            row_term(jnp.int32(0), lax.axis_size("mp") * own_rows).astype(jnp.bfloat16),
            "mp",
            scatter_dimension=0,
            tiled=True,
        )
        residual = (values.astype(jnp.float32) - targets[step_index].astype(jnp.float32)).astype(
            jnp.bfloat16
        )

        def add_rows(running, piece_rows, first_row, tokens=tokens):
            return lax.dot_general(
                tokens, piece_rows, (((0,), (0,)), ((), ())), preferred_element_type=jnp.float32
            )

        gradient = (
            add_rows(
                jnp.zeros(current.shape, jnp.float32),
                lax.all_gather(residual, "mp", axis=0, tiled=True),
                jnp.int32(0),
            )
            * grad_scale
        )
        velocity = momentum_decay * velocity + gradient
        half_step = current.astype(jnp.float32) - step_size * velocity
        kept_share = mix_share[0, step_index].astype(jnp.float32) / 8.0
        outgoing = ((1.0 - kept_share) * half_step).astype(jnp.bfloat16)
        outgoing_weight = ((1.0 - kept_share) * weight).astype(jnp.bfloat16)
        current = (kept_share * half_step + arrived.astype(jnp.float32)).astype(jnp.bfloat16)
        weight = kept_share * weight + arrived_weight
        message = (outgoing, outgoing_weight)
        if step_index == 0:
            message = from_behind((outgoing, outgoing_weight), "group", 1)
        else:
            message = from_behind((outgoing, outgoing_weight), "group", 2)
        arrived = message[0]
        arrived_weight = message[1].astype(jnp.float32)
        value_steps.append(values)
    return (current[None], weight, arrived[None], arrived_weight, jnp.stack(value_steps))


def solution(mesh):
    placed = (
        P(None, "group", "mp"),
        P(None, ("group", "mp"), None),
        P("group", "mp", None),
        P("group", "mp", None),
        P("group", "mp", None),
        P("group"),
        P("group"),
        P("group", None),
    )
    return jax.shard_map(
        local,
        mesh=mesh,
        in_specs=placed,
        out_specs=(
            P("group", "mp", None),
            P("group"),
            P("group", "mp", None),
            P("group"),
            P(None, ("group", "mp"), None),
        ),
        check_vma=False,
    )
```

profile of v0, /device:TPU:24, one launch (start us, length us, event | category | flops | bytes accessed | tf_op | source)
XLA Modules:
  0.0 253.6 jit_solution(1586570568530993772)
XLA Ops:
  7.2 2.9 %copy.21 = bf16[1,1024,1024]{1,2,0:T(8,128)(2,1)S(1)} copy(bf16[1,1024,1024]{2,1,0:T(8,128)(2,1)} %param.10) | data formatting | bytes 4194304 | tf_op args[2]
  10.7 4.4 %fusion.21 = bf16[768,1024]{0,1:T(8,128)(2,1)} fusion(bf16[1,1024,1024]{1,2,0:T(8,128)(2,1)S(1)} %copy.21, f32[]{:T(128)} %bitcast.89, bf16[2,768,1024]{2,1,0:T(8,128)(2,1)} %param.8), kind=kOutput, calls=%fused_computation.27 | convolution fusion | flops 1615331328 | bytes 5243392 | tf_op jit(solution)/shard_map/dot_general | solution.py:38
  15.2 2.7 %copy.31 = bf16[768,1024]{1,0:T(8,128)(2,1)} copy(bf16[768,1024]{0,1:T(8,128)(2,1)} %fusion.21) | data formatting | bytes 3145728
  18.0 0.2 copy.35
  18.1 31.3 %reduce-scatter.7.cloned.1.call-done = bf16[96,1024]{1,0:T(8,128)(2,1)} async-done(((bf16[768,1024]{1,0:T(8,128)(2,1)}), bf16[96,1024]{1,0:T(8,128)(2,1)}) %reduce-scatter.7.cloned.1.call-update) | async-done | bytes 196624
  49.5 1.1 copy.32
  50.6 0.1 fusion.36
  50.6 0.8 copy.24
  51.6 0.6 fusion.40
  52.8 5.5 %copy.22 = f32[1,1024,1024]{1,2,0:T(8,128)} copy(f32[1,1024,1024]{2,1,0:T(8,128)} %param.11) | data formatting | bytes 8388608 | tf_op args[3]
  59.0 2.6 %copy.25 = bf16[1,1024,1024]{1,2,0:T(8,128)(2,1)} copy(bf16[1,1024,1024]{2,1,0:T(8,128)(2,1)S(1)} %copy-done) | data formatting | bytes 4194304 | tf_op args[4]
  61.5 15.7 %all-gather.3.cloned.1.call-done = bf16[768,1024]{1,0:T(8,128)(2,1)} async-done(((bf16[96,1024]{1,0:T(8,128)(2,1)}), bf16[768,1024]{1,0:T(8,128)(2,1)}) %all-gather.3.cloned.1.call-update) | async-done | bytes 1572880 | tf_op jit(solution)/shard_map/all_gather | solution.py:59
  77.2 7.8 %multiply_convert_fusion.1 = (bf16[1024,1024]{0,1:T(8,128)(2,1)}, f32[1024,1024]{0,1:T(8,128)S(1)}) fusion(bf16[1,1024,1024]{1,2,0:T(8,128)(2,1)} %copy-done.1, f32[]{:T(128)} %sub.24, bf16[768,1024]{1,0:T(8,128)(2,1)} %all-gather.3.cloned.1.call-done, bf16[2,768,1024]{2,1,0:T(8,128)(2,1)} %param.8, f32[1,1024,1024]{1,2,0:T(8,128)} %copy.22), kind=kOutput, calls=%fused_computation.14 | convolution fusion | flops 1619001344 | bytes 15729152 | tf_op jit(solution)/shard_map/dot_general | solution.py:52
  85.1 1.9 copy-done.7
  87.0 3.5 %fusion.26 = bf16[768,1024]{0,1:T(8,128)(2,1)} fusion(f32[]{:T(128)} %bitcast.12, bf16[2,768,1024]{2,1,0:T(8,128)(2,1)S(1)} %copy-done.6, f32[1024,1024]{0,1:T(8,128)S(1)} %get-tuple-element.22, bf16[1,1024,1024]{1,2,0:T(8,128)(2,1)S(1)} %copy-done.2, bf16[1,1024,1024]{1,2,0:T(8,128)(2,1)S(1)} %copy-done.3, f32[]{:T(128)} %bitcast.1), kind=kOutput, calls=%fused_computation.28 | convolution fusion | flops 1622671360 | bytes 11534344 | tf_op jit(solution)/shard_map/dot_general | solution.py:38
  90.6 2.6 %copy.33 = bf16[768,1024]{1,0:T(8,128)(2,1)} copy(bf16[768,1024]{0,1:T(8,128)(2,1)} %fusion.26) | data formatting | bytes 3145728
  93.2 0.2 copy.36
  93.4 31.3 %reduce-scatter.9.cloned.1.call-done = bf16[96,1024]{1,0:T(8,128)(2,1)} async-done(((bf16[768,1024]{1,0:T(8,128)(2,1)}), bf16[96,1024]{1,0:T(8,128)(2,1)}) %reduce-scatter.9.cloned.1.call-update) | async-done | bytes 196624
  124.7 1.1 copy.34
  125.8 0.1 fusion.35
  125.9 0.8 copy.27
  126.8 1.3 collective-permute-start
  128.7 47.9 %collective-permute-done = bf16[1024,1024]{0,1:T(8,128)(2,1)} collective-permute-done((bf16[1024,1024]{0,1:T(8,128)(2,1)}, bf16[1024,1024]{0,1:T(8,128)(2,1)}, u32[]{:S(2)}, u32[]{:S(2)}) %collective-permute-start) | collective-permute-done | bytes 2097184 | tf_op jit(solution)/shard_map/ppermute | solution.py:19
  176.6 10.0 %multiply_convert_fusion = (bf16[1024,1024]{0,1:T(8,128)(2,1)}, bf16[1,1024,1024]{1,2,0:T(8,128)(2,1)}) fusion(f32[]{:T(128)} %sub.25, bf16[1024,1024]{0,1:T(8,128)(2,1)} %collective-permute-done, f32[]{:T(128)} %bitcast, bf16[768,1024]{1,0:T(8,128)(2,1)} %all-gather.5.cloned.1.call-done, bf16[2,768,1024]{2,1,0:T(8,128)(2,1)} %param.8, ...), kind=kOutput, calls=%fused_computation.12 | convolution fusion | flops 1630535680 | bytes 17827328 | tf_op jit(solution)/shard_map/dot_general | solution.py:52
  186.6 1.1 collective-permute-start.2
  187.6 1.7 collective-permute-start.1
  189.4 43.8 %collective-permute-start.3 = (bf16[1]{0:T(256)(128)(2,1)}, bf16[1]{0:T(256)(128)(2,1)}, u32[]{:S(2)}, u32[]{:S(2)}) collective-permute-start(bf16[1]{0:T(256)(128)(2,1)} %mul.109), channel_id=1, source_target_pairs={{0,16},{8,24},{16,0},{24,8},{1,17},{9,25},{17,1},{25,9},{2,18},{10... | collective-permute-start | bytes 14 | tf_op jit(solution)/shard_map/ppermute | solution.py:19
  233.1 1.4 collective-permute-done.3
  235.8 0.1 pad_maximum_fusion
  235.9 1.0 copy.30
  236.9 3.9 %copy.28 = bf16[1,1024,1024]{2,1,0:T(8,128)(2,1)} copy(bf16[1,1024,1024]{1,2,0:T(8,128)(2,1)} %get-tuple-element.16) | data formatting | bytes 4194304
  240.8 3.9 %copy.29 = bf16[1,1024,1024]{2,1,0:T(8,128)(2,1)} copy(bf16[1,1024,1024]{1,2,0:T(8,128)(2,1)} %bitcast.20) | data formatting | bytes 4194304
  (27 shorter events, 0.3 us)
Async XLA Ops:
  7.2 42.3 %reduce-scatter.7.cloned.1.call-start = ((), (), s32[]{:S(2)}) async-start(), calls=%async_computation.4 | async-start | bytes 1769472
  10.1 5.1 %copy-start.1 = (bf16[1,1024,1024]{1,2,0:T(8,128)(2,1)}, bf16[1,1024,1024]{1,2,0:T(8,128)(2,1)S(1)}, u32[]{:S(2)}) copy-start(bf16[1,1024,1024]{1,2,0:T(8,128)(2,1)S(1)} %copy.21) | copy-start | bytes 6291460
  15.2 2.7 %copy-start.4 = (bf16[2,96,1024]{2,1,0:T(8,128)(2,1)S(1)}, bf16[2,96,1024]{2,1,0:T(8,128)(2,1)}, u32[]{:S(2)}) copy-start(bf16[2,96,1024]{2,1,0:T(8,128)(2,1)} %param.9) | copy-start | bytes 1179652
  17.8 33.7 %copy-start.5 = (s32[1,2]{1,0:T(1,128)S(1)}, s32[1,2]{1,0:T(1,128)}, u32[]{:S(2)}) copy-start(s32[1,2]{1,0:T(1,128)} %param.15) | copy-start | bytes 28
  17.9 59.4 %all-gather.3.cloned.1.call-start = ((), (), s32[]{:S(2)}) async-start(), calls=%async_computation.2 | async-start | bytes 1769472 | tf_op jit(solution)/shard_map/all_gather | solution.py:59
  51.5 73.3 %reduce-scatter.9.cloned.1.call-start = ((), (), s32[]{:S(2)}) async-start(), calls=%async_computation.5 | async-start | bytes 1769472
  52.8 6.2 %copy-start = (bf16[1,1024,1024]{2,1,0:T(8,128)(2,1)S(1)}, bf16[1,1024,1024]{2,1,0:T(8,128)(2,1)}, u32[]{:S(2)}) copy-start(bf16[1,1024,1024]{2,1,0:T(8,128)(2,1)} %param.12) | copy-start | bytes 6291460
  61.5 25.5 %copy-start.2 = (bf16[1,1024,1024]{1,2,0:T(8,128)(2,1)S(1)}, bf16[1,1024,1024]{1,2,0:T(8,128)(2,1)}, u32[]{:S(2)}) copy-start(bf16[1,1024,1024]{1,2,0:T(8,128)(2,1)} %copy-done.1) | copy-start | bytes 6291460
  77.2 9.8 %copy-start.3 = (bf16[1,1024,1024]{1,2,0:T(8,128)(2,1)S(1)}, bf16[1,1024,1024]{1,2,0:T(8,128)(2,1)}, u32[]{:S(2)}) copy-start(bf16[1,1024,1024]{1,2,0:T(8,128)(2,1)} %copy.25) | copy-start | bytes 6291460
  77.2 9.8 %copy-start.6 = (bf16[2,768,1024]{2,1,0:T(8,128)(2,1)S(1)}, bf16[2,768,1024]{2,1,0:T(8,128)(2,1)}, u32[]{:S(2)}) copy-start(bf16[2,768,1024]{2,1,0:T(8,128)(2,1)} %param.8) | copy-start | bytes 9437188
  85.1 1.9 copy-start.7
  93.2 83.4 %all-gather.5.cloned.1.call-start = ((), (), s32[]{:S(2)}) async-start(), calls=%async_computation.3 | async-start | bytes 1769472 | tf_op jit(solution)/shard_map/all_gather | solution.py:59
  126.8 49.8 %collective-permute-start = (bf16[1024,1024]{0,1:T(8,128)(2,1)}, bf16[1024,1024]{0,1:T(8,128)(2,1)}, u32[]{:S(2)}, u32[]{:S(2)}) collective-permute-start(bf16[1024,1024]{0,1:T(8,128)(2,1)} %get-tuple-element.21), channel_id=1, source_target_pairs={{0,8},{8,16},{16,24},{24,0},{1,9},{9,17},{17,25},{25,1},{2,10},{10... | collective-permute-start | bytes 6291464 | tf_op jit(solution)/shard_map/ppermute | solution.py:19
  186.6 54.3 %collective-permute-start.2 = (bf16[1024,1024]{0,1:T(8,128)(2,1)}, bf16[1024,1024]{0,1:T(8,128)(2,1)}, u32[]{:S(2)}, u32[]{:S(2)}) collective-permute-start(bf16[1024,1024]{0,1:T(8,128)(2,1)} %get-tuple-element.15), channel_id=1, source_target_pairs={{0,16},{8,24},{16,0},{24,8},{1,17},{9,25},{17,1},{25,9},{2,18},{10... | collective-permute-start | bytes 6291464 | tf_op jit(solution)/shard_map/ppermute | solution.py:19
  187.6 47.5 %collective-permute-start.1 = (bf16[1]{0:T(256)(128)(2,1)}, bf16[1]{0:T(256)(128)(2,1)}, u32[]{:S(2)}, u32[]{:S(2)}) collective-permute-start(bf16[1]{0:T(256)(128)(2,1)} %mul.105), channel_id=1, source_target_pairs={{0,8},{8,16},{16,24},{24,0},{1,9},{9,17},{17,25},{25,1},{2,10},{10... | collective-permute-start | bytes 14 | tf_op jit(solution)/shard_map/ppermute | solution.py:19
  189.4 45.2 %collective-permute-start.3 = (bf16[1]{0:T(256)(128)(2,1)}, bf16[1]{0:T(256)(128)(2,1)}, u32[]{:S(2)}, u32[]{:S(2)}) collective-permute-start(bf16[1]{0:T(256)(128)(2,1)} %mul.109), channel_id=1, source_target_pairs={{0,16},{8,24},{16,0},{24,8},{1,17},{9,25},{17,1},{25,9},{2,18},{10... | collective-permute-start | bytes 14 | tf_op jit(solution)/shard_map/ppermute | solution.py:19
Sparse Core Ops, SparseCore 0:
  18.0 31.4 reduce-scatter.6
  51.7 25.5 all-gather.2
  93.3 31.4 reduce-scatter.8
  126.9 25.2 all-gather.4
where the time goes:
time: 254 us
  waiting for transfers between devices  128 us (50%)
  starting transfers between devices  48.1 us (19%)
  local copies, waits for them, and re-layouts  31.7 us (12%)
  matrix products  25.8 us (10%)
  between operations  20 us (8%)
    unnamed x6, waiting for transfers between devices  62.7 us
    ppermute x4, waiting for transfers between devices, from_behind(): return lax.ppermute(value, axis, pairs)  49.3 us
    ppermute x4, starting transfers between devices, from_behind(): return lax.ppermute(value, axis, pairs)  47.9 us
    unnamed x28, local copies, waits for them, and re-layouts  29.5 us
    dot_general x2, matrix products, add_rows(): lax.dot_general(tokens, piece_rows, (((0,), (0,)), ((), ())), preferred_e...  17.8 us
    all_gather x2, waiting for transfers between devices, local(): lax.all_gather(residual, 'mp', axis=0, tiled=True)  15.7 us
    dot_general x2, matrix products, row_term(): jnp.dot(tokens, scaled, preferred_element_type=jnp.float32) * row_scale  7.98 us
  transfers between devices with their start and end apart: 8, of which 5 were waited for; matrix products, arithmetic and copies ran while one was open for 6% of the time, Pallas kernels for 0%

commit v1 on v0

v1 whole, which is shorter than its diff:
```python
import functools
import math

import jax
import jax.numpy as jnp
from jax import lax
from jax.experimental import pallas as pl
from jax.experimental.pallas import tpu as pltpu
from jax.sharding import PartitionSpec as P

D = 8192
TOK_GRP = 768

momentum_decay = 0.9
step_size = 0.5
MESH = pl.DeviceIdType.MESH
f32, bf16 = jnp.float32, jnp.bfloat16


def kernel(
    n_group, n_mp, chunks, steps,
    pw_ref, rw_ref, mix_ref, x_hbm, tgt_hbm, num_hbm, mom_hbm, rec_hbm,
    fnum_hbm, frec_hbm, vr_hbm, fw_ref, frw_ref,
    x, xt, cur, vel, arr, tgt, part, sib, pair, peers, res, out, sc, val, wsend, wrecv,
    load_sem, sib_send, sib_recv, rs_send, rs_recv, ag_send, ag_recv, fwd_send, fwd_recv,
    msg_send, msg_recv, w_send, w_recv, store_sem,
):
    row_scale = 1.0 / math.sqrt(D)
    grad_scale = 1.0 / math.sqrt(TOK_GRP)
    nz = n_mp // 2
    rows, width = x.shape[1], x.shape[2]
    own = rows // n_mp
    cols = cur.shape[2]
    jobs = steps * chunks
    g = lax.axis_index("group")
    m = lax.axis_index("mp")
    z = m // 2
    core = m % 2
    other = 1 - core
    sibling = z * 2 + other

    def z_peer(d):
        return lax.rem(z + d, nz) * 2 + core

    def g_peer(d):
        return lax.rem(g + d + n_group, n_group)

    def span(c):
        return pl.ds(c * cols, cols)

    loads = {}

    def load(name, src, dst):
        copy = pltpu.make_async_copy(src, dst, load_sem.at[len(loads)])
        copy.start()
        loads[name] = copy

    load("num0", num_hbm.at[0, :, span(0)], cur.at[0])
    load("x0", x_hbm.at[0], x.at[0])
    for c in range(1, chunks):
        load(f"num{c}", num_hbm.at[0, :, span(c)], cur.at[c])
    for c in range(chunks):
        for s in range(steps):
            load(f"tgt{s}_{c}", tgt_hbm.at[s, :, span(c)], tgt.at[s * chunks + c])
    for c in range(chunks):
        load(f"mom{c}", mom_hbm.at[0, :, span(c)], vel.at[c])
        load(f"rec{c}", rec_hbm.at[0, :, span(c)], arr.at[c])
    for s in range(1, steps):
        load(f"x{s}", x_hbm.at[s], x.at[s])

    barrier = pltpu.get_barrier_semaphore()
    offsets = []
    for s in range(steps):
        for d in (2**s, -(2**s)):
            if d % n_group and d % n_group not in offsets:
                offsets.append(d % n_group)
    for d in offsets:
        pl.semaphore_signal(barrier, inc=1, device_id={"group": g_peer(d)}, device_id_type=MESH)
    for d in range(1, nz):
        pl.semaphore_signal(barrier, inc=1, device_id={"mp": z_peer(d)}, device_id_type=MESH)
    pl.semaphore_signal(barrier, inc=1, device_id={"mp": sibling}, device_id_type=MESH)
    pl.semaphore_wait(barrier, len(offsets) + nz)

    keep = [mix_ref[0, s].astype(f32) / 8.0 for s in range(steps)]
    weights = [pw_ref[0], keep[0] * pw_ref[0] + rw_ref[0]]
    w_copies = []
    for s in range(steps):
        outgoing_weight = jnp.full(wsend.shape[1:], (1.0 - keep[s]) * weights[s], f32)
        wsend[s] = outgoing_weight.astype(bf16).astype(f32)
        copy = pltpu.make_async_remote_copy(
            wsend.at[s], wrecv.at[s], w_send.at[s], w_recv.at[s],
            device_id={"group": g_peer(2**s)}, device_id_type=MESH,
        )
        copy.start()
        w_copies.append(copy)

    sends, stores = [], []
    sib_c, rs_c, ag_c, fwd_c, msg_c = {}, {}, {}, {}, {}

    def remote(src, dst, send, recv, where):
        copy = pltpu.make_async_remote_copy(src, dst, send, recv, device_id=where, device_id_type=MESH)
        copy.start()
        sends.append(copy)
        return copy

    def forward(j):
        s, c = divmod(j, chunks)
        if s == 0:
            loads[f"num{c}"].wait()
        if j == 0:
            loads["x0"].wait()
        sc[...] = (cur[c].astype(f32) / weights[s]).astype(bf16)
        half_z = nz // 2
        tile = half_z * 2 * own

        def body(i, _):
            lhs = x[s, pl.ds(pl.multiple_of(i * tile, tile), tile), :]
            product = jnp.dot(lhs, sc[...], preferred_element_type=f32) * row_scale
            part[j, pl.ds(i * half_z, half_z)] = product.astype(bf16).reshape(half_z, 2, own, cols)
            return 0

        lax.fori_loop(0, 2, body, 0)
        sib_c[j] = remote(part.at[j, :, other], sib.at[j], sib_send.at[j], sib_recv.at[j], {"mp": sibling})

    def pair_sum(j):
        sib_c[j].wait_recv()
        for k in range(nz):
            pair[j, k] = (part[j, k, core].astype(f32) + sib[j, k].astype(f32)).astype(bf16)
        for d in range(1, nz):
            rs_c[j, d] = remote(
                pair.at[j, lax.rem(z + d, nz)], peers.at[j, d - 1],
                rs_send.at[j, d - 1], rs_recv.at[j, d - 1], {"mp": z_peer(d)},
            )

    def value(j):
        s, c = divmod(j, chunks)
        total = pair[j, z].astype(f32)
        for d in range(1, nz):
            rs_c[j, d].wait_recv()
            total += peers[j, d - 1].astype(f32)
        values = total.astype(bf16)
        val[j] = values
        loads[f"tgt{s}_{c}"].wait()
        res[j, z, core] = (values.astype(f32) - tgt[j].astype(f32)).astype(bf16)
        for d in range(1, nz):
            ag_c[j, d] = remote(
                res.at[j, z, core], res.at[j, z, core],
                ag_send.at[j, d - 1], ag_recv.at[j, d - 1], {"mp": z_peer(d)},
            )
        store = pltpu.make_async_copy(val.at[j], vr_hbm.at[s, :, span(c)], store_sem.at[j])
        store.start()
        stores.append(store)

    def pass_on(j):
        for d in range(1, nz):
            source = lax.rem(z - d + nz, nz)
            pltpu.make_async_remote_copy(
                res.at[j, z, core], res.at[j, source, core],
                ag_send.at[j, d - 1], ag_recv.at[j, d - 1],
                device_id={"mp": z_peer(d)}, device_id_type=MESH,
            ).wait_recv()
        remote(res.at[j, :, core], res.at[j, :, core], fwd_send.at[j], fwd_recv.at[j], {"mp": sibling})

    def update(j):
        s, c = divmod(j, chunks)
        pltpu.make_async_remote_copy(
            res.at[j, :, core], res.at[j, :, other], fwd_send.at[j], fwd_recv.at[j],
            device_id={"mp": sibling}, device_id_type=MESH,
        ).wait_recv()
        if s == 0:
            loads[f"mom{c}"].wait()
            loads[f"rec{c}"].wait()
        else:
            msg_c[j - chunks].wait_recv()
        tile = min(256, width)

        def body(i, _):
            at = pl.ds(pl.multiple_of(i * tile, tile), tile)
            gradient = jnp.dot(
                xt[s, at, :], res[j].reshape(rows, cols), preferred_element_type=f32
            ) * grad_scale
            velocity = momentum_decay * vel[c, at, :] + gradient
            vel[c, at, :] = velocity
            half_step = cur[c, at, :].astype(f32) - step_size * velocity
            out[j, at, :] = ((1.0 - keep[s]) * half_step).astype(bf16)
            landed = arr[c, at, :] if s == 0 else arr[chunks + c, at, :]
            cur[c, at, :] = (keep[s] * half_step + landed.astype(f32)).astype(bf16)
            return 0

        lax.fori_loop(0, width // tile, body, 0)
        target = arr.at[chunks + c] if s == 0 else frec_hbm.at[0, :, span(c)]
        msg_c[j] = remote(out.at[j], target, msg_send.at[j], msg_recv.at[j], {"group": g_peer(2**s)})
        if s == steps - 1:
            store = pltpu.make_async_copy(cur.at[c], fnum_hbm.at[0, :, span(c)], store_sem.at[jobs + c])
            store.start()
            stores.append(store)

    def transpose(s):
        if s > 0:
            loads[f"x{s}"].wait()
        tile = min(256, width)
        for i in range(width // tile):
            xt[s, i * tile:(i + 1) * tile, :] = x[s, :, i * tile:(i + 1) * tile].T

    stages = (forward, pair_sum, value, pass_on, update)
    for tick in range(jobs + len(stages) - 1):
        for k in reversed(range(len(stages))):
            j = tick - k
            if 0 <= j < jobs:
                stages[k](j)
        if tick == 0:
            transpose(0)
        if tick == 2:
            for s in range(1, steps):
                transpose(s)

    for copy in w_copies:
        copy.wait()
    fw_ref[...] = keep[1] * weights[1] + wrecv[0]
    frw_ref[...] = wrecv[1]
    for c in range(chunks):
        msg_c[(steps - 1) * chunks + c].wait_recv()
    for copy in sends:
        copy.wait_send()
    for store in stores:
        store.wait()


def local(inputs, targets, numerator, momentum, received, push_weight, received_weight, mix_share):
    steps, rows, width = inputs.shape
    own, kv = targets.shape[1], targets.shape[2]
    n_group, n_mp = lax.axis_size("group"), lax.axis_size("mp")
    chunks = 4
    cols = kv // chunks
    jobs = steps * chunks
    nz = n_mp // 2
    any_space = pl.BlockSpec(memory_space=pl.ANY)
    smem = pl.BlockSpec(memory_space=pltpu.SMEM)
    vmem = pl.BlockSpec(memory_space=pltpu.VMEM)
    dma = pltpu.SemaphoreType.DMA
    fnum, frec, vr, fw, frw = pl.pallas_call(
        functools.partial(kernel, n_group, n_mp, chunks, steps),
        out_shape=(
            jax.ShapeDtypeStruct(numerator.shape, bf16),
            jax.ShapeDtypeStruct(numerator.shape, bf16),
            jax.ShapeDtypeStruct(targets.shape, bf16),
            jax.ShapeDtypeStruct((8, 128), f32),
            jax.ShapeDtypeStruct((8, 128), f32),
        ),
        in_specs=[smem] * 3 + [any_space] * 5,
        out_specs=(any_space, any_space, any_space, vmem, vmem),
        scratch_shapes=[
            pltpu.VMEM((steps, rows, width), bf16),
            pltpu.VMEM((steps, width, rows), bf16),
            pltpu.VMEM((chunks, width, cols), bf16),
            pltpu.VMEM((chunks, width, cols), f32),
            pltpu.VMEM((2 * chunks, width, cols), bf16),
            pltpu.VMEM((jobs, own, cols), bf16),
            pltpu.VMEM((jobs, nz, 2, own, cols), bf16),
            pltpu.VMEM((jobs, nz, own, cols), bf16),
            pltpu.VMEM((jobs, nz, own, cols), bf16),
            pltpu.VMEM((jobs, nz - 1, own, cols), bf16),
            pltpu.VMEM((jobs, nz, 2, own, cols), bf16),
            pltpu.VMEM((jobs, width, cols), bf16),
            pltpu.VMEM((width, cols), bf16),
            pltpu.VMEM((jobs, own, cols), bf16),
            pltpu.VMEM((steps, 8, 128), f32),
            pltpu.VMEM((steps, 8, 128), f32),
            dma((3 * chunks + steps * chunks + steps,)),
            dma((jobs,)), dma((jobs,)),
            dma((jobs, nz - 1)), dma((jobs, nz - 1)),
            dma((jobs, nz - 1)), dma((jobs, nz - 1)),
            dma((jobs,)), dma((jobs,)),
            dma((jobs,)), dma((jobs,)),
            dma((steps,)), dma((steps,)),
            dma((jobs + chunks,)),
        ],
        compiler_params=pltpu.CompilerParams(
            collective_id=0, has_side_effects=True, vmem_limit_bytes=58 * 1024 * 1024
        ),
    )(push_weight, received_weight, mix_share, inputs, targets, numerator, momentum, received)
    return fnum, fw[0, :1], frec, frw[0, :1], vr


def solution(mesh):
    placed = (
        P(None, "group", "mp"),
        P(None, ("group", "mp"), None),
        P("group", "mp", None),
        P("group", "mp", None),
        P("group", "mp", None),
        P("group"),
        P("group"),
        P("group", None),
    )
    return jax.shard_map(
        local,
        mesh=mesh,
        in_specs=placed,
        out_specs=(
            P("group", "mp", None),
            P("group"),
            P("group", "mp", None),
            P("group"),
            P(None, ("group", "mp"), None),
        ),
        check_vma=False,
    )
```

time: 254 us -> 129 us (0.51)
  waiting for transfers between devices: 128 us -> 0 us
  Pallas kernels: 0 us -> 118 us
  starting transfers between devices: 48.1 us -> 0 us
  matrix products: 25.8 us -> 0 us
  local copies, waits for them, and re-layouts: 31.7 us -> 7.68 us
  between operations: 20 us -> 1.94 us
    pallas_call x0 -> x1, Pallas kernels: none -> 118 us  [local(): pl.pallas_call(functools.partial(kernel, n_group, n_mp, chunks, steps), o...]
    unnamed x6 -> x0, waiting for transfers between devices: 62.7 us -> none
    ppermute x4 -> x0, waiting for transfers between devices: 49.3 us -> none  [from_behind(): return lax.ppermute(value, axis, pairs)]
    ppermute x4 -> x0, starting transfers between devices: 47.9 us -> none  [from_behind(): return lax.ppermute(value, axis, pairs)]
    dot_general x4 -> x0, matrix products: 25.8 us -> none  [the longest x2 17.8 us: add_rows(): lax.dot_general(tokens, piece_rows, (((0,), (0,)), ((), ())), preferred_e...]
    unnamed x28 -> x7, local copies, waits for them, and re-layouts: 29.5 us -> 5.3 us
    all_gather x2 -> x0, waiting for transfers between devices: 15.7 us -> none  [local(): lax.all_gather(residual, 'mp', axis=0, tiled=True)]
  transfers between devices with their start and end apart: 8 -> 0, of which waited for: 5 -> 0; matrix products, arithmetic and copies ran while one was open for 6% -> 0% of each run, Pallas kernels for 0% -> 0%
where the time goes in v1:
time: 129 us; the launch traced here: 128 us
  Pallas kernels  118 us (91%)
  local copies, waits for them, and re-layouts  7.68 us (6%)
  between operations  1.94 us (2%)
    pallas_call x1, Pallas kernels, local(): pl.pallas_call(functools.partial(kernel, n_group, n_mp, chunks, steps), o...  118 us
    unnamed x7, local copies, waits for them, and re-layouts  5.3 us

profile of v1, /device:TPU:24, one launch (start us, length us, event | category | flops | bytes accessed | tf_op | source)
XLA Modules:
  0.0 128.0 jit_solution(6302051617511184512)
XLA Ops:
  1.9 118.3 %shard_map.119 = (bf16[1,1024,1024]{2,1,0:T(8,128)(2,1)}, bf16[1,1024,1024]{2,1,0:T(8,128)(2,1)}, bf16[2,96,1024]{2,1,0:T(8,128)(2,1)}, f32[8,128]{1,0:T(8,128)}, f32[8,128]{1,0:T(8,128)}) custom-call(f32[1]{0:T(128)S(6)} %copy.16.pw_ref, f32[1]{0:T(128)S(6)} %copy.17.rw_ref, s32[1,2]{1,0:T(1,128)} %mix_ref.1, bf16[2,768,1024]{2,1,0:T(8,128)(2,1)} %x_hbm.1, ...), custom_call_target="tpu_custom_call" | custom-call | tf_op jit(solution)/shard_map/pallas_call | solution.py:241
  120.3 1.2 slice.7
  121.5 1.2 slice.6
  122.6 0.0 copy-start
  122.7 3.2 %copy.18 = bf16[1,1024,1024]{2,1,0:T(8,128)(2,1)} copy(bf16[1,1024,1024]{2,1,0:T(8,128)(2,1)} %get-tuple-element.20) | data formatting | bytes 4194304
  125.9 0.0 copy-done
  125.9 0.0 copy-start.1
  125.9 1.3 %copy.19 = bf16[1,1024,1024]{2,1,0:T(8,128)(2,1)} copy(bf16[1,1024,1024]{2,1,0:T(8,128)(2,1)S(1)} %copy-done) | data formatting | bytes 4194304
  127.2 0.0 copy-done.1
  127.2 0.7 copy.20
Async XLA Ops:
  122.6 3.2 %copy-start = (bf16[1,1024,1024]{2,1,0:T(8,128)(2,1)S(1)}, bf16[1,1024,1024]{2,1,0:T(8,128)(2,1)}, u32[]{:S(2)}) copy-start(bf16[1,1024,1024]{2,1,0:T(8,128)(2,1)} %get-tuple-element.22) | copy-start | bytes 6291460
  125.9 1.3 %copy-start.1 = (bf16[2,96,1024]{2,1,0:T(8,128)(2,1)S(1)}, bf16[2,96,1024]{2,1,0:T(8,128)(2,1)}, u32[]{:S(2)}) copy-start(bf16[2,96,1024]{2,1,0:T(8,128)(2,1)} %get-tuple-element.24) | copy-start | bytes 1179652

commit v2 on v1

--- a/solution.py
+++ b/solution.py
@@ -23,7 +23,7 @@
     fnum_hbm, frec_hbm, vr_hbm, fw_ref, frw_ref,
     x, xt, cur, vel, arr, tgt, part, sib, pair, peers, res, out, sc, val, wsend, wrecv,
     load_sem, sib_send, sib_recv, rs_send, rs_recv, ag_send, ag_recv, fwd_send, fwd_recv,
-    msg_send, msg_recv, w_send, w_recv, store_sem,
+    msg_send, msg_recv, relay_send, w_send, w_recv, store_sem,
 ):
     row_scale = 1.0 / math.sqrt(D)
     grad_scale = 1.0 / math.sqrt(TOK_GRP)
@@ -37,6 +37,11 @@
     z = m // 2
     core = m % 2
     other = 1 - core
+    odd = g % 2
+
+    def relayed(c):
+        return n_group % 2 == 0 and n_group > 2 and c % 2 == 1
+
     sibling = z * 2 + other
 
     def z_peer(d):
@@ -59,9 +64,8 @@
     load("x0", x_hbm.at[0], x.at[0])
     for c in range(1, chunks):
         load(f"num{c}", num_hbm.at[0, :, span(c)], cur.at[c])
-    for c in range(chunks):
-        for s in range(steps):
-            load(f"tgt{s}_{c}", tgt_hbm.at[s, :, span(c)], tgt.at[s * chunks + c])
+    for s in range(steps):
+        load(f"tgt{s}", tgt_hbm.at[s], tgt.at[s])
     for c in range(chunks):
         load(f"mom{c}", mom_hbm.at[0, :, span(c)], vel.at[c])
         load(f"rec{c}", rec_hbm.at[0, :, span(c)], arr.at[c])
@@ -139,17 +143,20 @@
             rs_c[j, d].wait_recv()
             total += peers[j, d - 1].astype(f32)
         values = total.astype(bf16)
-        val[j] = values
-        loads[f"tgt{s}_{c}"].wait()
-        res[j, z, core] = (values.astype(f32) - tgt[j].astype(f32)).astype(bf16)
+        columns = slice(c * cols, (c + 1) * cols)
+        val[s, :, columns] = values
+        if c == 0:
+            loads[f"tgt{s}"].wait()
+        res[j, z, core] = (values.astype(f32) - tgt[s, :, columns].astype(f32)).astype(bf16)
         for d in range(1, nz):
             ag_c[j, d] = remote(
                 res.at[j, z, core], res.at[j, z, core],
                 ag_send.at[j, d - 1], ag_recv.at[j, d - 1], {"mp": z_peer(d)},
             )
-        store = pltpu.make_async_copy(val.at[j], vr_hbm.at[s, :, span(c)], store_sem.at[j])
-        store.start()
-        stores.append(store)
+        if c == chunks - 1:
+            store = pltpu.make_async_copy(val.at[s], vr_hbm.at[s], store_sem.at[s])
+            store.start()
+            stores.append(store)
 
     def pass_on(j):
         for d in range(1, nz):
@@ -171,7 +178,7 @@
             loads[f"mom{c}"].wait()
             loads[f"rec{c}"].wait()
         else:
-            msg_c[j - chunks].wait_recv()
+            landing(j - chunks).wait_recv()
         tile = min(256, width)
 
         def body(i, _):
@@ -188,49 +195,101 @@
             return 0
 
         lax.fori_loop(0, width // tile, body, 0)
-        target = arr.at[chunks + c] if s == 0 else frec_hbm.at[0, :, span(c)]
-        msg_c[j] = remote(out.at[j], target, msg_send.at[j], msg_recv.at[j], {"group": g_peer(2**s)})
+        if s == 0 and relayed(c):
+            msg_c[j] = remote(
+                out.at[j], arr.at[chunks + c + odd * chunks], msg_send.at[j],
+                msg_recv.at[j + odd * jobs], {"group": g_peer(1 + odd)},
+            )
+        else:
+            msg_c[j] = remote(
+                out.at[j], arr.at[chunks + c if s == 0 else 3 * chunks + c],
+                msg_send.at[j], msg_recv.at[j], {"group": g_peer(2**s)},
+            )
         if s == steps - 1:
-            store = pltpu.make_async_copy(cur.at[c], fnum_hbm.at[0, :, span(c)], store_sem.at[jobs + c])
+            store = pltpu.make_async_copy(cur.at[c], fnum_hbm.at[0, :, span(c)], store_sem.at[steps + c])
             store.start()
             stores.append(store)
 
-    def transpose(s):
-        if s > 0:
+    def landing(j):
+        s, c = divmod(j, chunks)
+        return pltpu.make_async_remote_copy(
+            out.at[j], arr.at[chunks + c if s == 0 else 3 * chunks + c],
+            msg_send.at[j], msg_recv.at[j],
+            device_id={"group": g_peer(2**s)}, device_id_type=MESH,
+        )
+
+    def relay_copy(c):
+        return pltpu.make_async_remote_copy(
+            arr.at[2 * chunks + c], arr.at[chunks + c], relay_send.at[c], msg_recv.at[c],
+            device_id={"group": g_peer(-1)}, device_id_type=MESH,
+        )
+
+    def relay(c):
+        @pl.when(odd == 1)
+        def _():
+            pltpu.make_async_remote_copy(
+                out.at[c], arr.at[2 * chunks + c], msg_send.at[c], msg_recv.at[c + jobs],
+                device_id={"group": g_peer(2)}, device_id_type=MESH,
+            ).wait_recv()
+            relay_copy(c).start()
+
+    def transpose(s, i, pieces):
+        if s > 0 and i == 0:
             loads[f"x{s}"].wait()
-        tile = min(256, width)
-        for i in range(width // tile):
-            xt[s, i * tile:(i + 1) * tile, :] = x[s, :, i * tile:(i + 1) * tile].T
-
+        tile = width // pieces
+        xt[s, i * tile:(i + 1) * tile, :] = x[s, :, i * tile:(i + 1) * tile].T
+
+    relay_tick = 7
     stages = (forward, pair_sum, value, pass_on, update)
     for tick in range(jobs + len(stages) - 1):
         for k in reversed(range(len(stages))):
             j = tick - k
             if 0 <= j < jobs:
                 stages[k](j)
-        if tick == 0:
-            transpose(0)
-        if tick == 2:
-            for s in range(1, steps):
-                transpose(s)
+        if 0 <= tick - relay_tick < chunks and relayed(tick - relay_tick):
+            relay(tick - relay_tick)
+        for s in range(steps):
+            if 0 <= tick - s * chunks // 2 < 4:
+                transpose(s, tick - s * chunks // 2, 4)
 
     for copy in w_copies:
         copy.wait()
     fw_ref[...] = keep[1] * weights[1] + wrecv[0]
     frw_ref[...] = wrecv[1]
     for c in range(chunks):
-        msg_c[(steps - 1) * chunks + c].wait_recv()
+        landing((steps - 1) * chunks + c).wait_recv()
+        store = pltpu.make_async_copy(
+            arr.at[3 * chunks + c], frec_hbm.at[0, :, span(c)], store_sem.at[steps + chunks + c]
+        )
+        store.start()
+        stores.append(store)
     for copy in sends:
         copy.wait_send()
+    for c in range(chunks):
+        if relayed(c):
+            @pl.when(odd == 1)
+            def _():
+                relay_copy(c).wait_send()
     for store in stores:
         store.wait()
+
+
+def finish(fnum, frec, vr, fw, frw, fnum_out, fw_out, frec_out, frw_out, vr_out, sem):
+    copies = []
+    for i, (src, dst) in enumerate(((fnum, fnum_out), (frec, frec_out), (vr, vr_out))):
+        copies.append(pltpu.make_async_copy(src, dst, sem.at[i]))
+        copies[-1].start()
+    fw_out[0] = fw[0, 0]
+    frw_out[0] = frw[0, 0]
+    for copy in copies:
+        copy.wait()
 
 
 def local(inputs, targets, numerator, momentum, received, push_weight, received_weight, mix_share):
     steps, rows, width = inputs.shape
     own, kv = targets.shape[1], targets.shape[2]
     n_group, n_mp = lax.axis_size("group"), lax.axis_size("mp")
-    chunks = 4
+    chunks = 8
     cols = kv // chunks
     jobs = steps * chunks
     nz = n_mp // 2
@@ -254,8 +313,8 @@
             pltpu.VMEM((steps, width, rows), bf16),
             pltpu.VMEM((chunks, width, cols), bf16),
             pltpu.VMEM((chunks, width, cols), f32),
-            pltpu.VMEM((2 * chunks, width, cols), bf16),
-            pltpu.VMEM((jobs, own, cols), bf16),
+            pltpu.VMEM((4 * chunks, width, cols), bf16),
+            pltpu.VMEM((steps, own, kv), bf16),
             pltpu.VMEM((jobs, nz, 2, own, cols), bf16),
             pltpu.VMEM((jobs, nz, own, cols), bf16),
             pltpu.VMEM((jobs, nz, own, cols), bf16),
@@ -263,23 +322,35 @@
             pltpu.VMEM((jobs, nz, 2, own, cols), bf16),
             pltpu.VMEM((jobs, width, cols), bf16),
             pltpu.VMEM((width, cols), bf16),
-            pltpu.VMEM((jobs, own, cols), bf16),
+            pltpu.VMEM((steps, own, kv), bf16),
             pltpu.VMEM((steps, 8, 128), f32),
             pltpu.VMEM((steps, 8, 128), f32),
-            dma((3 * chunks + steps * chunks + steps,)),
+            dma((3 * chunks + 2 * steps,)),
             dma((jobs,)), dma((jobs,)),
             dma((jobs, nz - 1)), dma((jobs, nz - 1)),
             dma((jobs, nz - 1)), dma((jobs, nz - 1)),
             dma((jobs,)), dma((jobs,)),
-            dma((jobs,)), dma((jobs,)),
+            dma((jobs,)), dma((2 * jobs,)), dma((chunks,)),
             dma((steps,)), dma((steps,)),
-            dma((jobs + chunks,)),
+            dma((steps + 2 * chunks,)),
         ],
         compiler_params=pltpu.CompilerParams(
             collective_id=0, has_side_effects=True, vmem_limit_bytes=58 * 1024 * 1024
         ),
     )(push_weight, received_weight, mix_share, inputs, targets, numerator, momentum, received)
-    return fnum, fw[0, :1], frec, frw[0, :1], vr
+    return pl.pallas_call(
+        finish,
+        out_shape=(
+            jax.ShapeDtypeStruct(numerator.shape, bf16),
+            jax.ShapeDtypeStruct(push_weight.shape, f32),
+            jax.ShapeDtypeStruct(numerator.shape, bf16),
+            jax.ShapeDtypeStruct(push_weight.shape, f32),
+            jax.ShapeDtypeStruct(targets.shape, bf16),
+        ),
+        in_specs=[any_space, any_space, any_space, vmem, vmem],
+        out_specs=(any_space, smem, any_space, smem, any_space),
+        scratch_shapes=[dma((3,))],
+    )(fnum, frec, vr, fw, frw)
 
 
 def solution(mesh):

time: 129 us -> 262 us (2.03)
  Pallas kernels: 118 us -> 259 us
  local copies, waits for them, and re-layouts: 7.68 us -> 0 us
    pallas_call x0 -> x1, Pallas kernels: none -> 141 us  [local(): pl.pallas_call(finish, out_shape=(jax.ShapeDtypeStruct(numerator.shape, b...]
    unnamed x7 -> x0, local copies, waits for them, and re-layouts: 5.3 us -> none
where the time goes in v2:
time: 262 us; the launch traced here: 261 us
  Pallas kernels  259 us (99%)
    pallas_call x1, Pallas kernels, local(): pl.pallas_call(finish, out_shape=(jax.ShapeDtypeStruct(numerator.shape, b...  141 us
    pallas_call x1, Pallas kernels, local(): pl.pallas_call(functools.partial(kernel, n_group, n_mp, chunks, steps), o...  118 us

profile of v2, /device:TPU:24, one launch (start us, length us, event | category | flops | bytes accessed | tf_op | source)
XLA Modules:
  0.0 260.8 jit_solution(7820143336550835010)
XLA Ops:
  1.9 117.6 %shard_map.119 = (bf16[1,1024,1024]{2,1,0:T(8,128)(2,1)}, bf16[1,1024,1024]{2,1,0:T(8,128)(2,1)}, bf16[2,96,1024]{2,1,0:T(8,128)(2,1)}, f32[8,128]{1,0:T(8,128)}, f32[8,128]{1,0:T(8,128)}) custom-call(f32[1]{0:T(128)S(6)} %copy.13.pw_ref, f32[1]{0:T(128)S(6)} %copy.14.rw_ref, s32[1,2]{1,0:T(1,128)} %mix_ref.1, bf16[2,768,1024]{2,1,0:T(8,128)(2,1)} %x_hbm.1, ...), custom_call_target="tpu_custom_call" | custom-call | tf_op jit(solution)/shard_map/pallas_call | solution.py:300
  119.5 141.3 %shard_map.120 = (bf16[1,1024,1024]{2,1,0:T(8,128)(2,1)}, f32[1]{0:T(128)}, bf16[1,1024,1024]{2,1,0:T(8,128)(2,1)}, f32[1]{0:T(128)}, bf16[2,96,1024]{2,1,0:T(8,128)(2,1)}) custom-call(bf16[1,1024,1024]{2,1,0:T(8,128)(2,1)} %get-tuple-element.10.fnum, bf16[1,1024,1024]{2,1,0:T(8,128)(2,1)} %get-tuple-element.11.frec, ...), custom_call_target="tpu_custom_call" | custom-call | tf_op jit(solution)/shard_map/pallas_call | solution.py:341

commit v3 on v2

--- a/solution.py
+++ b/solution.py
@@ -239,15 +239,23 @@
         tile = width // pieces
         xt[s, i * tile:(i + 1) * tile, :] = x[s, :, i * tile:(i + 1) * tile].T
 
-    relay_tick = 7
-    stages = (forward, pair_sum, value, pass_on, update)
-    for tick in range(jobs + len(stages) - 1):
-        for k in reversed(range(len(stages))):
-            j = tick - k
-            if 0 <= j < jobs:
-                stages[k](j)
-        if 0 <= tick - relay_tick < chunks and relayed(tick - relay_tick):
-            relay(tick - relay_tick)
+    stages = ((update, 6), (pass_on, 5), (value, 3), (pair_sum, 1), (forward, 0))
+    depth = stages[0][1]
+    first, second = list(range(chunks)), list(range(chunks, jobs))
+    order = first[:depth]
+    first = first[depth:]
+    while second:
+        order.append(second.pop(0))
+        if first:
+            order.append(first.pop(0))
+    place = {j: i for i, j in enumerate(order)}
+    for tick in range(jobs + depth):
+        for stage, delay in stages:
+            if 0 <= tick - delay < jobs:
+                stage(order[tick - delay])
+        for c in range(chunks):
+            if relayed(c) and tick == place[c] + depth + 3:
+                relay(c)
         for s in range(steps):
             if 0 <= tick - s * chunks // 2 < 4:
                 transpose(s, tick - s * chunks // 2, 4)
@@ -274,15 +282,26 @@
         store.wait()
 
 
-def finish(fnum, frec, vr, fw, frw, fnum_out, fw_out, frec_out, frw_out, vr_out, sem):
-    copies = []
-    for i, (src, dst) in enumerate(((fnum, fnum_out), (frec, frec_out), (vr, vr_out))):
-        copies.append(pltpu.make_async_copy(src, dst, sem.at[i]))
-        copies[-1].start()
+def finish(fnum, frec, vr, fw, frw, fnum_out, fw_out, frec_out, frw_out, vr_out, hold, vr_hold, load_sem, store_sem):
+    moves = []
+    pieces, tile = hold.shape[1], hold.shape[2]
+    for i, (src, dst) in enumerate(((fnum, fnum_out), (frec, frec_out))):
+        for p in range(pieces):
+            at = pl.ds(p * tile, tile)
+            moves.append((src.at[0, at], hold.at[i, p], dst.at[0, at]))
+    moves.append((vr, vr_hold, vr_out))
+    loads, stores = [], []
+    for i, (src, via, dst) in enumerate(moves):
+        loads.append(pltpu.make_async_copy(src, via, load_sem.at[i]))
+        stores.append(pltpu.make_async_copy(via, dst, store_sem.at[i]))
+        loads[-1].start()
     fw_out[0] = fw[0, 0]
     frw_out[0] = frw[0, 0]
-    for copy in copies:
-        copy.wait()
+    for load, store in zip(loads, stores):
+        load.wait()
+        store.start()
+    for store in stores:
+        store.wait()
 
 
 def local(inputs, targets, numerator, momentum, received, push_weight, received_weight, mix_share):
@@ -293,6 +312,7 @@
     cols = kv // chunks
     jobs = steps * chunks
     nz = n_mp // 2
+    pieces = 4
     any_space = pl.BlockSpec(memory_space=pl.ANY)
     smem = pl.BlockSpec(memory_space=pltpu.SMEM)
     vmem = pl.BlockSpec(memory_space=pltpu.VMEM)
@@ -349,7 +369,12 @@
         ),
         in_specs=[any_space, any_space, any_space, vmem, vmem],
         out_specs=(any_space, smem, any_space, smem, any_space),
-        scratch_shapes=[dma((3,))],
+        scratch_shapes=[
+            pltpu.VMEM((2, pieces, width // pieces, kv), bf16),
+            pltpu.VMEM(targets.shape, bf16),
+            dma((2 * pieces + 1,)), dma((2 * pieces + 1,)),
+        ],
+        compiler_params=pltpu.CompilerParams(vmem_limit_bytes=16 * 1024 * 1024),
     )(fnum, frec, vr, fw, frw)
 
 

time: 262 us -> 117 us (0.45)
  Pallas kernels: 259 us -> 109 us
  local copies, waits for them, and re-layouts: 0 us -> 5.54 us
    pallas_call x1, Pallas kernels: 141 us -> 3.31 us  [local(): pl.pallas_call(finish, out_shape=(jax.ShapeDtypeStruct(numerator.shape, b...]
    pallas_call x1, Pallas kernels: 118 us -> 106 us  [local(): pl.pallas_call(functools.partial(kernel, n_group, n_mp, chunks, steps), o...]
    unnamed x0 -> x10, local copies, waits for them, and re-layouts: none -> 5.54 us
where the time goes in v3:
time: 117 us; the launch traced here: 116 us
  Pallas kernels  109 us (93%)
  local copies, waits for them, and re-layouts  5.54 us (5%)
  between operations  1.95 us (2%)
    pallas_call x1, Pallas kernels, local(): pl.pallas_call(functools.partial(kernel, n_group, n_mp, chunks, steps), o...  106 us
    unnamed x10, local copies, waits for them, and re-layouts  5.54 us
    pallas_call x1, Pallas kernels, local(): pl.pallas_call(finish, out_shape=(jax.ShapeDtypeStruct(numerator.shape, b...  3.31 us

profile of v3, /device:TPU:24, one launch (start us, length us, event | category | flops | bytes accessed | tf_op | source)
XLA Modules:
  0.0 116.4 jit_solution(6094127183623742712)
XLA Ops:
  1.9 105.6 %shard_map.119 = (bf16[1,1024,1024]{2,1,0:T(8,128)(2,1)}, bf16[1,1024,1024]{2,1,0:T(8,128)(2,1)}, bf16[2,96,1024]{2,1,0:T(8,128)(2,1)}, f32[8,128]{1,0:T(8,128)}, f32[8,128]{1,0:T(8,128)}) custom-call(f32[1]{0:T(128)S(6)} %copy.13.pw_ref, f32[1]{0:T(128)S(6)} %copy.14.rw_ref, s32[1,2]{1,0:T(1,128)} %mix_ref.1, bf16[2,768,1024]{2,1,0:T(8,128)(2,1)} %x_hbm.1, ...), custom_call_target="tpu_custom_call" | custom-call | tf_op jit(solution)/shard_map/pallas_call | solution.py:320
  107.5 0.0 copy-start
  107.6 1.6 %copy-done = bf16[1,1024,1024]{2,1,0:T(8,128)(2,1)S(1)} copy-done((bf16[1,1024,1024]{2,1,0:T(8,128)(2,1)S(1)}, bf16[1,1024,1024]{2,1,0:T(8,128)(2,1)}, u32[]{:S(2)}) %copy-start) | copy-done | bytes 2097176
  109.1 0.0 copy-start.1
  109.1 1.6 %copy-done.1 = bf16[1,1024,1024]{2,1,0:T(8,128)(2,1)S(1)} copy-done((bf16[1,1024,1024]{2,1,0:T(8,128)(2,1)S(1)}, bf16[1,1024,1024]{2,1,0:T(8,128)(2,1)}, u32[]{:S(2)}) %copy-start.1) | copy-done | bytes 2097176
  110.7 0.0 copy-start.2
  110.7 1.0 copy-done.2
  111.7 0.0 copy-start.3
  111.7 0.7 copy-done.3
  112.4 0.0 copy-start.4
  112.4 0.7 copy-done.4
  113.1 3.3 %shard_map.120 = (bf16[1,1024,1024]{2,1,0:T(8,128)(2,1)}, f32[1]{0:T(128)}, bf16[1,1024,1024]{2,1,0:T(8,128)(2,1)}, f32[1]{0:T(128)}, bf16[2,96,1024]{2,1,0:T(8,128)(2,1)}) custom-call(bf16[1,1024,1024]{2,1,0:T(8,128)(2,1)S(1)} %copy-done, bf16[1,1024,1024]{2,1,0:T(8,128)(2,1)S(1)} %copy-done.1, bf16[2,96,1024]{2,1,0:T(8,128)(2,1)S(1)} %copy-done.2, ...), custom_call_target="tpu_custom_call" | custom-call | tf_op jit(solution)/shard_map/pallas_call | solution.py:361
Async XLA Ops:
  107.5 1.6 %copy-start = (bf16[1,1024,1024]{2,1,0:T(8,128)(2,1)S(1)}, bf16[1,1024,1024]{2,1,0:T(8,128)(2,1)}, u32[]{:S(2)}) copy-start(bf16[1,1024,1024]{2,1,0:T(8,128)(2,1)} %get-tuple-element.10.fnum) | copy-start | bytes 6291460
  109.1 1.6 %copy-start.1 = (bf16[1,1024,1024]{2,1,0:T(8,128)(2,1)S(1)}, bf16[1,1024,1024]{2,1,0:T(8,128)(2,1)}, u32[]{:S(2)}) copy-start(bf16[1,1024,1024]{2,1,0:T(8,128)(2,1)} %get-tuple-element.11.frec) | copy-start | bytes 6291460
  110.7 1.0 copy-start.2
  111.7 0.7 copy-start.3
  112.4 0.7 copy-start.4

commit v4 on v3

--- a/solution.py
+++ b/solution.py
@@ -15,6 +15,17 @@
 step_size = 0.5
 MESH = pl.DeviceIdType.MESH
 f32, bf16 = jnp.float32, jnp.bfloat16
+CHUNKS = 8
+SCHEDULE = (
+    (0, 0), (0, 1), (0, 2), (1, 0), (1, 1), (0, 3), (1, 2), (5, 0), (5, 1), (5, 2), (1, 3), (2, 0),
+    (5, 3), (5, 4), (5, 5), (2, 1), (5, 6), (5, 7), (2, 2), (2, 3), (3, 0), (4, 0), (3, 1), (0, 8),
+    (3, 2), (0, 4), (4, 1), (4, 2), (3, 3), (1, 8), (1, 4), (0, 9), (4, 3), (0, 5), (2, 8), (6, 1),
+    (1, 9), (0, 10), (2, 4), (1, 5), (0, 6), (3, 8), (1, 10), (1, 6), (4, 8), (6, 3), (3, 4), (2, 9),
+    (0, 11), (4, 4), (2, 5), (2, 10), (1, 11), (0, 7), (2, 6), (3, 9), (1, 7), (4, 9), (3, 5), (0, 12),
+    (3, 10), (4, 5), (4, 10), (3, 6), (2, 11), (1, 12), (0, 13), (4, 6), (2, 7), (1, 13), (3, 11), (0, 14),
+    (6, 5), (2, 12), (4, 11), (3, 7), (1, 14), (2, 13), (4, 7), (3, 12), (0, 15), (4, 12), (2, 14), (3, 13),
+    (1, 15), (4, 13), (6, 7), (3, 14), (4, 14), (2, 15), (3, 15), (4, 15),
+)
 
 
 def kernel(
@@ -225,6 +236,9 @@
         )
 
     def relay(c):
+        if not relayed(c):
+            return
+
         @pl.when(odd == 1)
         def _():
             pltpu.make_async_remote_copy(
@@ -233,32 +247,16 @@
             ).wait_recv()
             relay_copy(c).start()
 
-    def transpose(s, i, pieces):
+    def transpose(index):
+        s, i = divmod(index, 4)
         if s > 0 and i == 0:
             loads[f"x{s}"].wait()
-        tile = width // pieces
+        tile = width // 4
         xt[s, i * tile:(i + 1) * tile, :] = x[s, :, i * tile:(i + 1) * tile].T
 
-    stages = ((update, 6), (pass_on, 5), (value, 3), (pair_sum, 1), (forward, 0))
-    depth = stages[0][1]
-    first, second = list(range(chunks)), list(range(chunks, jobs))
-    order = first[:depth]
-    first = first[depth:]
-    while second:
-        order.append(second.pop(0))
-        if first:
-            order.append(first.pop(0))
-    place = {j: i for i, j in enumerate(order)}
-    for tick in range(jobs + depth):
-        for stage, delay in stages:
-            if 0 <= tick - delay < jobs:
-                stage(order[tick - delay])
-        for c in range(chunks):
-            if relayed(c) and tick == place[c] + depth + 3:
-                relay(c)
-        for s in range(steps):
-            if 0 <= tick - s * chunks // 2 < 4:
-                transpose(s, tick - s * chunks // 2, 4)
+    stages = (forward, pair_sum, value, pass_on, update, transpose, relay)
+    for stage, index in SCHEDULE:
+        stages[stage](index)
 
     for copy in w_copies:
         copy.wait()
@@ -308,7 +306,7 @@
     steps, rows, width = inputs.shape
     own, kv = targets.shape[1], targets.shape[2]
     n_group, n_mp = lax.axis_size("group"), lax.axis_size("mp")
-    chunks = 8
+    chunks = CHUNKS
     cols = kv // chunks
     jobs = steps * chunks
     nz = n_mp // 2
@@ -374,7 +372,7 @@
             pltpu.VMEM(targets.shape, bf16),
             dma((2 * pieces + 1,)), dma((2 * pieces + 1,)),
         ],
-        compiler_params=pltpu.CompilerParams(vmem_limit_bytes=16 * 1024 * 1024),
+        compiler_params=pltpu.CompilerParams(vmem_limit_bytes=58 * 1024 * 1024),
     )(fnum, frec, vr, fw, frw)
 
 

time: 117 us -> 119 us (1.017)
  the two profiles are of different devices: /device:TPU:24 before, /device:TPU:27 now
where the time goes in v4:
time: 119 us
  Pallas kernels  117 us (98%)
  between operations  1.93 us (2%)
    pallas_call x1, Pallas kernels, local(): pl.pallas_call(functools.partial(kernel, n_group, n_mp, chunks, steps), o...  112 us
    pallas_call x1, Pallas kernels, local(): pl.pallas_call(finish, out_shape=(jax.ShapeDtypeStruct(numerator.shape, b...  5.18 us

profile of v4, /device:TPU:27, one launch (start us, length us, event | category | flops | bytes accessed | tf_op | source)
XLA Modules:
  0.0 119.1 jit_solution(17309750208317367449)
XLA Ops:
  1.9 112.0 %shard_map.119 = (bf16[1,1024,1024]{2,1,0:T(8,128)(2,1)}, bf16[1,1024,1024]{2,1,0:T(8,128)(2,1)}, bf16[2,96,1024]{2,1,0:T(8,128)(2,1)}, f32[8,128]{1,0:T(8,128)}, f32[8,128]{1,0:T(8,128)}) custom-call(f32[1]{0:T(128)S(6)} %copy.13.pw_ref, f32[1]{0:T(128)S(6)} %copy.14.rw_ref, s32[1,2]{1,0:T(1,128)} %mix_ref.1, bf16[2,768,1024]{2,1,0:T(8,128)(2,1)} %x_hbm.1, ...), custom_call_target="tpu_custom_call" | custom-call | tf_op jit(solution)/shard_map/pallas_call | solution.py:318
  113.9 5.2 %shard_map.120 = (bf16[1,1024,1024]{2,1,0:T(8,128)(2,1)}, f32[1]{0:T(128)}, bf16[1,1024,1024]{2,1,0:T(8,128)(2,1)}, f32[1]{0:T(128)}, bf16[2,96,1024]{2,1,0:T(8,128)(2,1)}) custom-call(bf16[1,1024,1024]{2,1,0:T(8,128)(2,1)} %get-tuple-element.10.fnum, bf16[1,1024,1024]{2,1,0:T(8,128)(2,1)} %get-tuple-element.11.frec, ...), custom_call_target="tpu_custom_call" | custom-call | tf_op jit(solution)/shard_map/pallas_call | solution.py:359

commit v5 on v3

--- a/solution.py
+++ b/solution.py
@@ -123,7 +123,7 @@
             part[j, pl.ds(i * half_z, half_z)] = product.astype(bf16).reshape(half_z, 2, own, cols)
             return 0
 
-        lax.fori_loop(0, 2, body, 0)
+        lax.fori_loop(0, 2, body, 0, unroll=True)
         sib_c[j] = remote(part.at[j, :, other], sib.at[j], sib_send.at[j], sib_recv.at[j], {"mp": sibling})
 
     def pair_sum(j):
@@ -187,14 +187,15 @@
                 xt[s, at, :], res[j].reshape(rows, cols), preferred_element_type=f32
             ) * grad_scale
             velocity = momentum_decay * vel[c, at, :] + gradient
-            vel[c, at, :] = velocity
+            if s < steps - 1:
+                vel[c, at, :] = velocity
             half_step = cur[c, at, :].astype(f32) - step_size * velocity
             out[j, at, :] = ((1.0 - keep[s]) * half_step).astype(bf16)
             landed = arr[c, at, :] if s == 0 else arr[chunks + c, at, :]
             cur[c, at, :] = (keep[s] * half_step + landed.astype(f32)).astype(bf16)
             return 0
 
-        lax.fori_loop(0, width // tile, body, 0)
+        lax.fori_loop(0, width // tile, body, 0, unroll=True)
         if s == 0 and relayed(c):
             msg_c[j] = remote(
                 out.at[j], arr.at[chunks + c + odd * chunks], msg_send.at[j],
@@ -312,7 +313,7 @@
     cols = kv // chunks
     jobs = steps * chunks
     nz = n_mp // 2
-    pieces = 4
+    pieces = 8
     any_space = pl.BlockSpec(memory_space=pl.ANY)
     smem = pl.BlockSpec(memory_space=pltpu.SMEM)
     vmem = pl.BlockSpec(memory_space=pltpu.VMEM)
@@ -374,7 +375,7 @@
             pltpu.VMEM(targets.shape, bf16),
             dma((2 * pieces + 1,)), dma((2 * pieces + 1,)),
         ],
-        compiler_params=pltpu.CompilerParams(vmem_limit_bytes=16 * 1024 * 1024),
+        compiler_params=pltpu.CompilerParams(vmem_limit_bytes=58 * 1024 * 1024),
     )(fnum, frec, vr, fw, frw)
 
 

time: 117 us -> 112 us (0.957)
  local copies, waits for them, and re-layouts: 5.54 us -> 0 us
    unnamed x10 -> x0, local copies, waits for them, and re-layouts: 5.54 us -> none
    pallas_call x1, Pallas kernels: 3.31 us -> 5.54 us  [local(): pl.pallas_call(finish, out_shape=(jax.ShapeDtypeStruct(numerator.shape, b...]
where the time goes in v5:
time: 112 us
  Pallas kernels  110 us (98%)
  between operations  2.09 us (2%)
    pallas_call x1, Pallas kernels, local(): pl.pallas_call(functools.partial(kernel, n_group, n_mp, chunks, steps), o...  105 us
    pallas_call x1, Pallas kernels, local(): pl.pallas_call(finish, out_shape=(jax.ShapeDtypeStruct(numerator.shape, b...  5.54 us

profile of v5, /device:TPU:24, one launch (start us, length us, event | category | flops | bytes accessed | tf_op | source)
XLA Modules:
  0.0 112.1 jit_solution(9768934445192345431)
XLA Ops:
  1.9 104.5 %shard_map.119 = (bf16[1,1024,1024]{2,1,0:T(8,128)(2,1)}, bf16[1,1024,1024]{2,1,0:T(8,128)(2,1)}, bf16[2,96,1024]{2,1,0:T(8,128)(2,1)}, f32[8,128]{1,0:T(8,128)}, f32[8,128]{1,0:T(8,128)}) custom-call(f32[1]{0:T(128)S(6)} %copy.13.pw_ref, f32[1]{0:T(128)S(6)} %copy.14.rw_ref, s32[1,2]{1,0:T(1,128)} %mix_ref.1, bf16[2,768,1024]{2,1,0:T(8,128)(2,1)} %x_hbm.1, ...), custom_call_target="tpu_custom_call" | custom-call | tf_op jit(solution)/shard_map/pallas_call | solution.py:321
  106.5 5.5 %shard_map.120 = (bf16[1,1024,1024]{2,1,0:T(8,128)(2,1)}, f32[1]{0:T(128)}, bf16[1,1024,1024]{2,1,0:T(8,128)(2,1)}, f32[1]{0:T(128)}, bf16[2,96,1024]{2,1,0:T(8,128)(2,1)}) custom-call(bf16[1,1024,1024]{2,1,0:T(8,128)(2,1)} %get-tuple-element.10.fnum, bf16[1,1024,1024]{2,1,0:T(8,128)(2,1)} %get-tuple-element.11.frec, ...), custom_call_target="tpu_custom_call" | custom-call | tf_op jit(solution)/shard_map/pallas_call | solution.py:362

commit v6 on v3

--- a/solution.py
+++ b/solution.py
@@ -187,7 +187,8 @@
                 xt[s, at, :], res[j].reshape(rows, cols), preferred_element_type=f32
             ) * grad_scale
             velocity = momentum_decay * vel[c, at, :] + gradient
-            vel[c, at, :] = velocity
+            if s < steps - 1:
+                vel[c, at, :] = velocity
             half_step = cur[c, at, :].astype(f32) - step_size * velocity
             out[j, at, :] = ((1.0 - keep[s]) * half_step).astype(bf16)
             landed = arr[c, at, :] if s == 0 else arr[chunks + c, at, :]
@@ -239,7 +240,7 @@
         tile = width // pieces
         xt[s, i * tile:(i + 1) * tile, :] = x[s, :, i * tile:(i + 1) * tile].T
 
-    stages = ((update, 6), (pass_on, 5), (value, 3), (pair_sum, 1), (forward, 0))
+    stages = ((update, 5), (pass_on, 4), (value, 2), (pair_sum, 1), (forward, 0))
     depth = stages[0][1]
     first, second = list(range(chunks)), list(range(chunks, jobs))
     order = first[:depth]
@@ -374,7 +375,7 @@
             pltpu.VMEM(targets.shape, bf16),
             dma((2 * pieces + 1,)), dma((2 * pieces + 1,)),
         ],
-        compiler_params=pltpu.CompilerParams(vmem_limit_bytes=16 * 1024 * 1024),
+        compiler_params=pltpu.CompilerParams(vmem_limit_bytes=58 * 1024 * 1024),
     )(fnum, frec, vr, fw, frw)
 
 

time: 117 us -> 128 us (1.094); the launches traced: 116 us -> 125 us
  Pallas kernels: 109 us -> 123 us
  local copies, waits for them, and re-layouts: 5.54 us -> 0 us
    pallas_call x1, Pallas kernels: 106 us -> 118 us  [local(): pl.pallas_call(functools.partial(kernel, n_group, n_mp, chunks, steps), o...]
    unnamed x10 -> x0, local copies, waits for them, and re-layouts: 5.54 us -> none
    pallas_call x1, Pallas kernels: 3.31 us -> 5.18 us  [local(): pl.pallas_call(finish, out_shape=(jax.ShapeDtypeStruct(numerator.shape, b...]
where the time goes in v6:
time: 128 us; the launch traced here: 125 us
  Pallas kernels  123 us (96%)
  between operations  1.93 us (2%)
    pallas_call x1, Pallas kernels, local(): pl.pallas_call(functools.partial(kernel, n_group, n_mp, chunks, steps), o...  118 us
    pallas_call x1, Pallas kernels, local(): pl.pallas_call(finish, out_shape=(jax.ShapeDtypeStruct(numerator.shape, b...  5.18 us

profile of v6, /device:TPU:24, one launch (start us, length us, event | category | flops | bytes accessed | tf_op | source)
XLA Modules:
  0.0 125.4 jit_solution(10190738605751297295)
XLA Ops:
  1.9 118.3 %shard_map.119 = (bf16[1,1024,1024]{2,1,0:T(8,128)(2,1)}, bf16[1,1024,1024]{2,1,0:T(8,128)(2,1)}, bf16[2,96,1024]{2,1,0:T(8,128)(2,1)}, f32[8,128]{1,0:T(8,128)}, f32[8,128]{1,0:T(8,128)}) custom-call(f32[1]{0:T(128)S(6)} %copy.13.pw_ref, f32[1]{0:T(128)S(6)} %copy.14.rw_ref, s32[1,2]{1,0:T(1,128)} %mix_ref.1, bf16[2,768,1024]{2,1,0:T(8,128)(2,1)} %x_hbm.1, ...), custom_call_target="tpu_custom_call" | custom-call | tf_op jit(solution)/shard_map/pallas_call | solution.py:321
  120.2 5.2 %shard_map.120 = (bf16[1,1024,1024]{2,1,0:T(8,128)(2,1)}, f32[1]{0:T(128)}, bf16[1,1024,1024]{2,1,0:T(8,128)(2,1)}, f32[1]{0:T(128)}, bf16[2,96,1024]{2,1,0:T(8,128)(2,1)}) custom-call(bf16[1,1024,1024]{2,1,0:T(8,128)(2,1)} %get-tuple-element.10.fnum, bf16[1,1024,1024]{2,1,0:T(8,128)(2,1)} %get-tuple-element.11.frec, ...), custom_call_target="tpu_custom_call" | custom-call | tf_op jit(solution)/shard_map/pallas_call | solution.py:362
